TPU v7x, 32 devices: a whole 2x2x4 slice. The times are simulated.
32 devices in a mesh: groups: 2 (over y), picks: 4 (over z), heads: 4 (over x, core).
Axes of the slice: x: 2, y: 2, z: 4, core: 2. Of those that a mesh axis runs over, the one named last changes fastest.
Arguments:
- coords: float32 [3, 8192], P(None, ('groups', 'picks')), parts along dimension 1, may hold values from -1 to 1
- horizon_ids: int32 [8192], P(('groups', 'picks')), parts along dimension 0, may hold values from 0 to 63
- horizon_levels: float32 [128], P('groups'), parts along dimension 0, may hold values from -2 to 2
- latents: bfloat16 [512, 1024], replicated, may hold values from -960 to 960
- kv_weight: bfloat16 [3072, 2, 1024], P('picks', None, 'heads'), may hold values from -0.109375 to 0.109375
- cross_out: bfloat16 [1024, 1024], P('heads'), may hold values from -0.75 to 0.75
- norm_gains: float32 [2, 1024], replicated, may hold values from 0.1 to 1.9
- self_qkv: bfloat16 [3, 1024, 1024], P(None, None, 'heads'), may hold values from -0.1875 to 0.1875
- self_out: bfloat16 [1024, 1024], P(None, 'heads'), may hold values from -0.1875 to 0.1875
- dec_kv: bfloat16 [2, 1024, 1024], P(None, None, 'heads'), may hold values from -0.1875 to 0.1875
- dec_query: bfloat16 [3072, 1024], P('picks', 'heads'), may hold values from -0.109375 to 0.109375
- readout: float32 [1024], P('heads'), may hold values from -0.1875 to 0.1875
Outputs:
- field: float32 [8192], P(('groups', 'picks')), parts along dimension 0
- latents_out: float32 [1024, 1024], P('groups', 'heads'), parts along dimension 0
- grad_query: float32 [6144, 1024], P(('groups', 'picks'), 'heads'), parts along dimension 0
There are 2 independent parts, one for each index of `groups`. A program takes and returns all parts, laid end to end along the dimension named above; an argument that names none is the same for every part. Nothing has to cross between parts.
All inputs are finite; a program needn't handle non-finite values.
Results may differ from a plain program's by a relative error of at most 0.028.
Values may be sent and summed in bfloat16 or wider, within the bound.
A program may use at most 64 MiB of HBM per device.

v0:
```python
import jax
import jax.numpy as jnp
from jax import lax
from jax.sharding import PartitionSpec as P

HEAD = 128
BANDS = 512
HORIZONS = 64


PI = 3.141592653589793
EPS = 1e-06


def encode(coords):
    freq = jnp.linspace(1.0, BANDS / 2.0, BANDS).astype(jnp.float32)
    angle = PI * freq[None, :, None] * coords[:, None, :]
    table = jnp.concatenate([jnp.sin(angle), jnp.cos(angle)], axis=0)
    return table.reshape(6 * BANDS, coords.shape[1]).T.astype(jnp.bfloat16)


def on_device(
    coords,
    horizon_ids,
    horizon_levels,
    latents,
    kv_weight,
    cross_out,
    norm_gains,
    self_qkv,
    self_out,
    dec_kv,
    dec_query,
    readout,
):
    high = lax.Precision.HIGHEST
    scale = HEAD ** (-0.5)
    count = coords.shape[1]
    width = latents.shape[1]
    lat_rows = latents.shape[0]
    local = kv_weight.shape[2]
    nheads = local // HEAD
    column = lax.axis_index("heads") * local
    enc = encode(coords)
    piece = lax.all_gather(kv_weight, "picks", axis=0, tiled=True)
    rows = enc
    keys_vals = jnp.dot(
        rows, piece.reshape(piece.shape[0], 2 * local), preferred_element_type=jnp.float32
    ).astype(jnp.bfloat16)
    keys = keys_vals[:, :local].reshape(count, nheads, HEAD)
    values = keys_vals[:, local:].reshape(count, nheads, HEAD)
    queries = lax.dynamic_slice_in_dim(latents, column, local, 1).reshape(lat_rows, nheads, HEAD)
    scores = jnp.einsum("lhc,thc->hlt", queries, keys, preferred_element_type=jnp.float32) * scale
    top = jnp.max(scores, axis=2)
    expo = jnp.exp(scores - top[:, :, None])
    total = jnp.sum(expo, axis=2)
    numer = jnp.einsum(
        "hlt,thc->hlc", expo.astype(jnp.bfloat16), values, preferred_element_type=jnp.float32
    )
    best = lax.pmax(top, "picks")
    factor = jnp.exp(top - best)
    total, numer = (
        lax.psum((total * factor).astype(jnp.bfloat16), "picks").astype(jnp.float32),
        lax.psum((numer * factor[:, :, None]).astype(jnp.bfloat16), "picks").astype(jnp.float32),
    )
    attended = (
        (numer / total[:, :, None]).transpose(1, 0, 2).reshape(lat_rows, local).astype(jnp.bfloat16)
    )
    gain_two = lax.dynamic_slice_in_dim(norm_gains[1], column, local, 0)
    partial_value = jnp.dot(attended, cross_out, preferred_element_type=jnp.float32)
    whole = latents.astype(jnp.float32) + lax.psum(
        partial_value.astype(jnp.bfloat16), "heads"
    ).astype(jnp.float32)
    power = jnp.mean(whole * whole, axis=1, keepdims=True)
    normed = (whole * lax.rsqrt(power + EPS) * norm_gains[0][None, :]).astype(jnp.bfloat16)
    state = lax.dynamic_slice_in_dim(whole, column, local, 1)
    qkv = jnp.einsum("ld,kde->kle", normed, self_qkv, preferred_element_type=jnp.float32).astype(
        jnp.bfloat16
    )
    self_q = qkv[0].reshape(lat_rows, nheads, HEAD)
    self_k = qkv[1].reshape(lat_rows, nheads, HEAD)
    self_v = qkv[2].reshape(lat_rows, nheads, HEAD)
    inner = jnp.einsum("lhc,mhc->hlm", self_q, self_k, preferred_element_type=jnp.float32) * scale
    raised = jnp.exp(inner)
    probs = (raised / jnp.sum(raised, axis=2, keepdims=True)).astype(jnp.bfloat16)
    head_out = (
        jnp.einsum("hlm,mhc->lhc", probs, self_v, preferred_element_type=jnp.float32)
        .astype(jnp.bfloat16)
        .reshape(lat_rows, local)
    )
    every_head = lax.all_gather(head_out, "heads", axis=1, tiled=True)
    latents_out = state + jnp.dot(every_head, self_out, preferred_element_type=jnp.float32)
    power_two = lax.psum(jnp.sum(latents_out * latents_out, axis=1), "heads")
    piece_two = (
        latents_out * lax.rsqrt(power_two / width + EPS)[:, None] * gain_two[None, :]
    ).astype(jnp.bfloat16)
    normed2 = lax.all_gather(piece_two, "heads", axis=1, tiled=True)
    dec = jnp.einsum("ld,kde->kle", normed2, dec_kv, preferred_element_type=jnp.float32).astype(
        jnp.bfloat16
    )
    dec_keys = dec[0].reshape(lat_rows, nheads, HEAD)
    dec_vals = dec[1].reshape(lat_rows, nheads, HEAD)
    rows = enc
    query = jnp.dot(
        rows,
        lax.all_gather(dec_query, "picks", axis=0, tiled=True),
        preferred_element_type=jnp.float32,
    ).astype(jnp.bfloat16)
    dec_q = query.reshape(count, nheads, HEAD)
    logits = jnp.einsum("thc,lhc->htl", dec_q, dec_keys, preferred_element_type=jnp.float32) * scale
    lifted = jnp.exp(logits)
    weights = lifted / jnp.sum(lifted, axis=2, keepdims=True)
    out = jnp.einsum(
        "htl,lhc->thc", weights.astype(jnp.bfloat16), dec_vals, preferred_element_type=jnp.float32
    )
    read = readout.reshape(nheads, HEAD)
    field = lax.psum(jnp.sum(out * read[None, :, :], axis=(1, 2)), "heads")
    onehot = (horizon_ids[:, None] == jnp.arange(HORIZONS, dtype=jnp.int32)[None, :]).astype(
        jnp.float32
    )
    target = jnp.sum(onehot * horizon_levels[None, :], axis=1)
    miss = field - target
    value_read = jnp.einsum("lhc,hc->hl", dec_vals.astype(jnp.float32), read, precision=high)
    dprob = miss[None, :, None] * value_read[:, None, :]
    dscore = (weights * (dprob - jnp.sum(dprob * weights, axis=2, keepdims=True))).astype(
        jnp.bfloat16
    )
    dquery = (
        (jnp.einsum("htl,lhc->thc", dscore, dec_keys, preferred_element_type=jnp.float32) * scale)
        .reshape(count, local)
        .astype(jnp.bfloat16)
    )
    rows = enc
    grad_query = lax.psum_scatter(
        jnp.dot(rows.T, dquery, preferred_element_type=jnp.float32).astype(jnp.bfloat16),
        "picks",
        scatter_dimension=0,
        tiled=True,
    ).astype(jnp.float32)
    return (field, latents_out, grad_query)


def solution(mesh):
    in_specs = (
        P(None, ("groups", "picks")),
        P(("groups", "picks")),
        P("groups"),
        P(),
        P("picks", None, "heads"),
        P("heads", None),
        P(),
        P(None, None, "heads"),
        P(None, "heads"),
        P(None, None, "heads"),
        P("picks", "heads"),
        P("heads"),
    )
    out_specs = (P(("groups", "picks")), P("groups", "heads"), P(("groups", "picks"), "heads"))
    return jax.shard_map(
        on_device, mesh=mesh, in_specs=in_specs, out_specs=out_specs, check_vma=False
    )
```

profile of v0, /device:TPU:8, one launch (start us, length us, event | category | flops | bytes accessed | tf_op | source)
XLA Modules:
  0.0 317.3 jit_solution(10722653969841569074)
XLA Ops:
  9.2 23.6 %fusion = (bf16[3,512,1024]{2,1,0:T(8,128)(2,1)S(1)}, bf16[3,512,1024]{2,1,0:T(8,128)(2,1)S(1)}) fusion(f32[3,1024]{1,0:T(4,128)} %param.12, f32[512]{0:T(512)S(1)} %maximum_multiply_fusion), kind=kLoop, calls=%fused_computation.2 | loop fusion | flops 4718592 | bytes 6305792 | tf_op jit(solution)/shard_map/convert
  32.8 3.2 %pad_maximum_fusion = bf16[6,512,1024]{2,1,0:T(8,128)(2,1)} fusion(bf16[3,512,1024]{2,1,0:T(8,128)(2,1)S(1)} %get-tuple-element.15, bf16[3,512,1024]{2,1,0:T(8,128)(2,1)S(1)} %get-tuple-element.14), kind=kLoop, calls=%fused_computation.4 | loop fusion | flops 3145728 | bytes 12582912 | tf_op jit(solution)/shard_map/concatenate | solution.py:18
  35.9 36.0 %all-gather.5.cloned.1.call-done = bf16[3072,2,256]{2,1,0:T(2,128)(2,1)} async-done(((bf16[768,2,256]{2,1,0:T(2,128)(2,1)}), bf16[3072,2,256]{2,1,0:T(2,128)(2,1)}) %all-gather.5.cloned.1.call-update) | async-done | bytes 3145744 | tf_op jit(solution)/shard_map/all_gather | solution.py:45
  72.0 2.6 copy.88
  74.6 1.1 copy-done.4
  75.7 3.5 %convolution_convert_fusion.2 = bf16[1024,512]{0,1:T(8,128)(2,1)S(1)} fusion(bf16[3072,1024]{1,0:T(8,128)(2,1)S(1)} %bitcast.66, bf16[3072,512]{1,0:T(8,128)(2,1)S(1)} %bitcast.71), kind=kOutput, calls=%fused_computation.34 | convolution fusion | flops 3221749760 | bytes 10485760 | tf_op jit(solution)/shard_map/dot_general | solution.py:47
  79.3 2.8 multiply_reduce_fusion
  82.1 11.2 %pmax.7 = f32[2,512]{1,0:T(2,128)S(1)} all-reduce(f32[2,512]{1,0:T(2,128)S(1)} %get-tuple-element.18), channel_id=1, replica_groups=mesh['groups'=2,'picks'=4,'heads'=4] {'picks'}, use_global_device_ids=true, to_apply=%region_1.2 | all-reduce | flops 1024 | bytes 8192 | tf_op jit(solution)/shard_map/pmax | solution.py:60
  93.3 3.2 %fusion.7 = f32[2,512]{1,0:T(2,128)S(1)} fusion(f32[2,512,1024]{2,1,0:T(8,128)} %get-tuple-element.19, f32[2,512]{1,0:T(2,128)S(1)} %get-tuple-element.18), kind=kLoop, calls=%fused_computation.16 | loop fusion | flops 3144704 | bytes 4202496 | tf_op jit(solution)/shard_map/reduce_sum | solution.py:56
  96.7 1.6 fusion.38
  98.4 9.1 %psum.36 = bf16[2,512]{1,0:T(2,128)(2,1)S(1)} all-reduce(bf16[2,512]{1,0:T(2,128)(2,1)S(1)} %get-tuple-element.3), channel_id=1, replica_groups=mesh['groups'=2,'picks'=4,'heads'=4] {'picks'}, use_global_device_ids=true, to_apply=%region_4.5 | all-reduce | flops 1024 | bytes 4096 | tf_op jit(solution)/shard_map/psum | solution.py:63
  107.5 25.3 %all-reduce.3.cloned.1.call-done = bf16[2,512,128]{2,1,0:T(8,128)(2,1)} async-done(((bf16[2,512,128]{2,1,0:T(8,128)(2,1)}), bf16[2,512,128]{2,1,0:T(8,128)(2,1)}) %all-reduce.3.cloned.1.call-update) | async-done | bytes 262160 | tf_op jit(solution)/shard_map/psum | solution.py:64
  132.9 1.2 fusion.46
  134.2 2.5 convolution_convert_fusion.1
  137.0 35.8 %all-reduce.5.cloned.1.call-done = bf16[512,1024]{1,0:T(8,128)(2,1)} async-done(((bf16[512,1024]{1,0:T(8,128)(2,1)}), bf16[512,1024]{1,0:T(8,128)(2,1)}) %all-reduce.5.cloned.1.call-update) | async-done | bytes 1048592 | tf_op jit(solution)/shard_map/psum | solution.py:71
  172.8 3.0 convert_add_fusion
  175.8 1.2 fusion.30
  177.5 1.2 convolution_convert_fusion.6
  179.5 16.6 %all-gather.7.cloned.1.call-done = bf16[512,1024]{0,1:T(8,128)(2,1)} async-done(((bf16[512,256]{0,1:T(8,128)(2,1)}), bf16[512,1024]{0,1:T(8,128)(2,1)}) %all-gather.7.cloned.1.call-update) | async-done | bytes 1048592 | tf_op jit(solution)/shard_map/all_gather | solution.py:91
  196.1 1.9 multiply_reduce_fusion.2
  198.0 6.1 %psum.38 = f32[512]{0:T(512)S(1)} all-reduce(f32[512]{0:T(512)S(1)} %get-tuple-element.22), channel_id=1, replica_groups=mesh['groups'=2,'picks'=4,'heads'=4] {'heads'}, use_global_device_ids=true, to_apply=%region_9.10 | all-reduce | flops 512 | bytes 4096 | tf_op jit(solution)/shard_map/psum | solution.py:93
  205.1 28.5 %all-gather.11.cloned.1.call-done = bf16[3072,256]{1,0:T(8,128)(2,1)} async-done(((bf16[768,256]{1,0:T(8,128)(2,1)}), bf16[3072,256]{1,0:T(8,128)(2,1)}) %all-gather.11.cloned.1.call-update) | async-done | bytes 1572880 | tf_op jit(solution)/shard_map/all_gather | solution.py:106
  233.6 5.1 %convolution_convert_fusion.4 = bf16[1024,256]{0,1:T(8,128)(2,1)S(1)} fusion(bf16[3072,1024]{1,0:T(8,128)(2,1)} %bitcast.65, bf16[3072,256]{1,0:T(8,128)(2,1)} %all-gather.11.cloned.1.call-done), kind=kOutput, calls=%fused_computation.38 | convolution fusion | flops 1610874880 | bytes 8388608 | tf_op jit(solution)/shard_map/dot_general | solution.py:104
  238.7 13.7 %all-gather.9.cloned.1.call-done = bf16[512,1024]{1,0:T(8,128)(2,1)} async-done(((bf16[512,256]{1,0:T(8,128)(2,1)}), bf16[512,1024]{1,0:T(8,128)(2,1)}) %all-gather.9.cloned.1.call-update) | async-done | bytes 1048592 | tf_op jit(solution)/shard_map/all_gather | solution.py:97
  252.3 2.3 fusion.34
  255.5 2.0 copy-done.1
  258.5 6.1 %psum.39 = f32[1024]{0:T(1024)S(1)} all-reduce(f32[1024]{0:T(1024)S(1)} %fusion.31), channel_id=1, replica_groups=mesh['groups'=2,'picks'=4,'heads'=4] {'heads'}, use_global_device_ids=true, to_apply=%region_12.13 | all-reduce | flops 1024 | bytes 8192 | tf_op jit(solution)/shard_map/psum | solution.py:117
  264.8 3.3 %fusion.2 = f32[2,1024]{1,0:T(2,128)S(1)} fusion(f32[2,512]{1,0:T(2,128)S(1)} %bitcast.85, f32[1024]{0:T(1024)S(1)} %sub.37, f32[2,1024]{1,0:T(2,128)S(1)} %get-tuple-element.24, f32[2,1024,512]{1,2,0:T(8,128)} %copy-done.1), kind=kLoop, calls=%fused_computation.7 | loop fusion | flops 5240832 | bytes 4218880 | tf_op jit(solution)/shard_map/reduce_sum | solution.py:125
  268.2 1.4 fusion.27
  270.1 3.1 convolution_convert_fusion
  273.3 35.2 %reduce-scatter.2.cloned.1.call-done = bf16[768,256]{1,0:T(8,128)(2,1)} async-done(((bf16[3072,256]{1,0:T(8,128)(2,1)}), bf16[768,256]{1,0:T(8,128)(2,1)}) %reduce-scatter.2.cloned.1.call-update) | async-done | bytes 393232 | tf_op jit(solution)/shard_map/reduce_scatter | solution.py:134
  308.5 1.9 convert_element_type.123
  (67 shorter events, 7.7 us)
Async XLA Ops:
  7.2 168.6 %copy-start = (bf16[3,1024,256]{2,1,0:T(8,128)(2,1)S(1)}, bf16[3,1024,256]{2,1,0:T(8,128)(2,1)}, u32[]{:S(2)}) copy-start(bf16[3,1024,256]{2,1,0:T(8,128)(2,1)} %param.19) | copy-start | bytes 4718596
  7.2 64.8 %all-gather.5.cloned.1.call-start = ((), (), s32[]{:S(2)}) async-start(), calls=%async_computation.1 | async-start | bytes 3932160 | tf_op jit(solution)/shard_map/all_gather | solution.py:45
  7.9 124.9 %all-reduce.3.cloned.1.call-start = ((), (), s32[]{:S(2)}) async-start(), calls=%async_computation.2 | async-start | bytes 524288 | tf_op jit(solution)/shard_map/psum | solution.py:64
  72.0 3.7 %copy-start.4 = (bf16[6,512,1024]{2,1,0:T(8,128)(2,1)S(1)}, bf16[6,512,1024]{2,1,0:T(8,128)(2,1)}, u32[]{:S(2)}) copy-start(bf16[6,512,1024]{2,1,0:T(8,128)(2,1)} %pad_maximum_fusion) | copy-start | bytes 18874372
  93.3 3.4 %copy-start.3 = (f32[2,512,1024]{2,1,0:T(8,128)S(1)}, f32[2,512,1024]{2,1,0:T(8,128)}, u32[]{:S(2)}) copy-start(f32[2,512,1024]{2,1,0:T(8,128)} %get-tuple-element.19) | copy-start | bytes 12582916
  96.7 40.2 %copy-start.9 = (f32[2,1024]{1,0:T(2,128)S(1)}, f32[2,1024]{1,0:T(2,128)}, u32[]{:S(2)}) copy-start(f32[2,1024]{1,0:T(2,128)} %param.18) | copy-start | bytes 24580
  96.7 76.1 %copy-start.5 = (bf16[512,1024]{1,0:T(8,128)(2,1)S(1)}, bf16[512,1024]{1,0:T(8,128)(2,1)}, u32[]{:S(2)}) copy-start(bf16[512,1024]{1,0:T(8,128)(2,1)} %param.15) | copy-start | bytes 3145732
  98.3 74.4 %all-reduce.5.cloned.1.call-start = ((), (), s32[]{:S(2)}) async-start(), calls=%async_computation.3 | async-start | bytes 2097152 | tf_op jit(solution)/shard_map/psum | solution.py:71
  136.7 59.4 %all-gather.7.cloned.1.call-start = ((), (), s32[]{:S(2)}) async-start(), calls=%async_computation.4 | async-start | bytes 1310720 | tf_op jit(solution)/shard_map/all_gather | solution.py:91
  172.8 3.0 copy-start.6
  177.5 18.5 %copy-start.13 = (bf16[1024,256]{1,0:T(8,128)(2,1)S(1)}, bf16[1024,256]{1,0:T(8,128)(2,1)}, u32[]{:S(2)}) copy-start(bf16[1024,256]{1,0:T(8,128)(2,1)} %param.20) | copy-start | bytes 1572868
  178.8 26.2 %copy-start.10 = (s32[1024]{0:T(1024)S(1)}, s32[1024]{0:T(1024)}, u32[]{:S(2)}) copy-start(s32[1024]{0:T(1024)} %param.13) | copy-start | bytes 12292
  178.8 26.2 %copy-start.12 = (f32[64]{0:T(128)S(1)}, f32[64]{0:T(128)}, u32[]{:S(2)}) copy-start(f32[64]{0:T(128)} %param.14) | copy-start | bytes 772
  178.8 54.8 %all-gather.11.cloned.1.call-start = ((), (), s32[]{:S(2)}) async-start(), calls=%async_computation.6 | async-start | bytes 1966080 | tf_op jit(solution)/shard_map/all_gather | solution.py:106
  179.4 72.9 %all-gather.9.cloned.1.call-start = ((), (), s32[]{:S(2)}) async-start(), calls=%async_computation.5 | async-start | bytes 1310720 | tf_op jit(solution)/shard_map/all_gather | solution.py:97
  198.0 40.7 %copy-start.7 = (f32[512,256]{1,0:T(8,128)}, f32[512,256]{1,0:T(8,128)S(1)}, u32[]{:S(2)}) copy-start(f32[512,256]{1,0:T(8,128)S(1)} %get-tuple-element.23) | copy-start | bytes 1572868
  204.9 103.6 %reduce-scatter.2.cloned.1.call-start = ((), (), s32[]{:S(2)}) async-start(), calls=%async_computation.7 | async-start | bytes 1966080 | tf_op jit(solution)/shard_map/reduce_scatter | solution.py:134
  238.7 18.9 %copy-start.11 = (f32[256]{0:T(256)S(1)}, f32[256]{0:T(256)}, u32[]{:S(2)}) copy-start(f32[256]{0:T(256)} %param.23) | copy-start | bytes 3076
  255.5 2.0 copy-start.1
  264.6 5.0 %copy-start.8 = (f32[1024]{0:T(1024)}, f32[1024]{0:T(1024)S(1)}, u32[]{:S(2)}) copy-start(f32[1024]{0:T(1024)S(1)} %psum.39) | copy-start | bytes 12292
  264.6 3.6 %copy-start.2 = (f32[2,1024,512]{1,2,0:T(8,128)S(1)}, f32[2,1024,512]{1,2,0:T(8,128)}, u32[]{:S(2)}) copy-start(f32[2,1024,512]{1,2,0:T(8,128)} %copy-done.1) | copy-start | bytes 12582916
  264.8 4.7 %slice-start = ((s8[6291456]{0:T(1024)(128)(4,1)}), s8[4194304]{0:T(1024)(128)(4,1)S(1)}, s32[]{:S(2)}) async-start(s8[6291456]{0:T(1024)(128)(4,1)} %bitcast.67), calls=%async_computation.8 | async-start | bytes 8388608
  268.2 2.0 slice-start.1
Sparse Core Ops, SparseCore 0:
  9.6 62.3 all-gather.4
  98.5 34.3 all-reduce.2
  136.8 35.8 all-reduce.4
  178.9 17.0 all-gather.6
  197.5 36.0 all-gather.10
  235.6 16.7 all-gather.8
  273.4 35.0 reduce-scatter.1
where the time goes:
time: 320 us; the launch traced here: 317 us
  waiting for transfers between devices  192 us (60%)
  other arithmetic  40.5 us (13%)
  blocking collectives  32.4 us (10%)
  matrix products  29.1 us (9%)
  between operations  14.4 us (4%)
  local copies, waits for them, and re-layouts  8.03 us (3%)
    all_gather x1, waiting for transfers between devices, on_device(): piece = lax.all_gather(kv_weight, 'picks', axis=0, tiled=True)  36 us
    psum x1, waiting for transfers between devices, on_device(): lax.psum(partial_value.astype(jnp.bfloat16), 'heads').astype(jnp.float32)  35.8 us
    reduce_scatter x1, waiting for transfers between devices, on_device(): lax.psum_scatter(jnp.dot(rows.T, dquery, preferred_element_type=jnp.float...  35.2 us
    all_gather x1, waiting for transfers between devices, on_device(): lax.all_gather(dec_query, 'picks', axis=0, tiled=True)  28.5 us
    psum x1, waiting for transfers between devices, on_device(): lax.psum((numer * factor[:, :, None]).astype(jnp.bfloat16), 'picks')  25.3 us
    another operation x1, other arithmetic  23.6 us
    all_gather x1, waiting for transfers between devices, on_device(): every_head = lax.all_gather(head_out, 'heads', axis=1, tiled=True)  16.6 us
    all_gather x1, waiting for transfers between devices, on_device(): normed2 = lax.all_gather(piece_two, 'heads', axis=1, tiled=True)  13.7 us
  transfers between devices with their start and end apart: 7, of which 7 were waited for; matrix products, arithmetic and copies ran while one was open for 11% of the time, Pallas kernels for 0%

commit v1 on v0

v1 whole, which is shorter than its diff:
```python
import functools

import jax
import jax.numpy as jnp
from jax import lax
from jax.experimental import pallas as pl
from jax.experimental.pallas import tpu as pltpu
from jax.sharding import PartitionSpec as P

HEAD = 128
BANDS = 512
HORIZONS = 64
PI = 3.141592653589793
EPS = 1e-06
F32 = jnp.float32
BF16 = jnp.bfloat16
LAST = (((1,), (1,)), ((), ()))


def sin_half(r):
    u = r * r
    p = 0.07765766 * u - 0.5982913
    p = p * u + 2.55007753
    p = p * u - 5.16771008
    p = p * u + PI
    return p * r


def cos_half(r):
    u = r * r
    p = -0.02439632 * u + 0.23493732
    p = p * u - 1.335212
    p = p * u + 4.05870916
    p = p * u - 4.93480214
    return p * u + 1.0


def kernel(
    npick, nhead,
    coords_ref, ids_ref, levels_ref, freq_ref, latents_ref, kv_in, cross_in, gains_ref,
    qkvw_ref, sout_in, deckv_ref, dq_in, readout_ref,
    field_ref, latout_ref, grad_ref,
    enc, kvw, dqw, cross, sout, kvs, numer, stats, stin, parts, coef, coeft, att, state,
    qkv, heads_all, dkeys, dkeyst, vread, query, dqt, dqb, fpart, fin, gbuf, gin,
    kv_s, kv_r, kvy_s, kvy_r, dq_s, dq_r, dqy_s, dqy_r, cr_s, cr_r, so_s, so_r,
    nu_s, nu_r, st_s, st_r, az_s, az_r, ah_s, ah_r, ho_s, ho_r, fd_s, fd_r, gr_s, gr_r, loc,
):
    g = lax.axis_index("groups")
    p = lax.axis_index("picks")
    hd = lax.axis_index("heads")
    mate = {"groups": 1 - g}
    scale = HEAD ** (-0.5)
    count, features = enc.shape
    lat_rows, width = latents_ref.shape
    rows = dq_in.shape[0]
    half = rows // 2
    local = dq_in.shape[1]
    nh = local // HEAD
    share = lat_rows // npick
    col = pl.multiple_of(hd * local, HEAD)
    sends = []

    def put(src, dst, ssem, rsem, to):
        return pltpu.make_async_remote_copy(
            src_ref=src, dst_ref=dst, send_sem=ssem, recv_sem=rsem, device_id=to,
            device_id_type=pl.DeviceIdType.MESH,
        )

    def go(copy):
        copy.start()
        sends.append(copy)
        return copy

    zto = [None] + [{"picks": lax.rem(p + d, npick)} for d in range(1, npick)]
    zfrom = [p] + [lax.rem(p + npick - d, npick) for d in range(1, npick)]
    hto = [None] + [{"heads": lax.rem(hd + e, nhead)} for e in range(1, nhead)]

    own = []
    mine = pl.multiple_of(p * rows, 16)
    own.append(pltpu.make_async_copy(kv_in, kvw.at[pl.ds(mine, rows)], loc.at[0]))
    own.append(pltpu.make_async_copy(dq_in, dqw.at[pl.ds(mine, rows)], loc.at[1]))
    own.append(pltpu.make_async_copy(cross_in, cross.at[pl.ds(col, local)], loc.at[2]))
    own.append(pltpu.make_async_copy(sout_in, sout.at[:, pl.ds(col, local)], loc.at[3]))
    for c in own:
        c.start()

    barrier = pltpu.get_barrier_semaphore()
    for to in zto[1:] + hto[1:] + [mate]:
        pl.semaphore_signal(barrier, inc=1, device_id=to, device_id_type=pl.DeviceIdType.MESH)
    pl.semaphore_wait(barrier, npick + nhead - 1)

    myhalf = pl.multiple_of(g * half, 16)
    dst_half = pl.ds(pl.multiple_of(p * rows + g * half, 16), half)
    kvz = [None] + [
        go(put(kv_in.at[pl.ds(myhalf, half)], kvw.at[dst_half], kv_s.at[d], kv_r.at[d], zto[d]))
        for d in range(1, npick)
    ]
    crh = [
        go(put(cross_in, cross.at[pl.ds(col, local)], cr_s.at[e], cr_r.at[e], hto[e]))
        for e in range(1, nhead)
    ]
    soh = [
        go(put(sout_in, sout.at[:, pl.ds(col, local)], so_s.at[e], so_r.at[e], hto[e]))
        for e in range(1, nhead)
    ]
    dqz = [None] + [
        go(put(dq_in.at[pl.ds(myhalf, half)], dqw.at[dst_half], dq_s.at[d], dq_r.at[d], zto[d]))
        for d in range(1, npick)
    ]

    tile = 32
    freq = freq_ref[...]

    def encode(i, _):
        at = pl.ds(pl.multiple_of(i * tile, tile), tile)
        for c in range(3):
            turn = coords_ref[at, c : c + 1] * freq
            r = turn - jnp.floor(turn + 0.5)
            s = sin_half(r)
            k = cos_half(r)
            enc[at, c * BANDS : (c + 1) * BANDS] = (2.0 * s * k).astype(BF16)
            enc[at, (3 + c) * BANDS : (4 + c) * BANDS] = (1.0 - 2.0 * s * s).astype(BF16)
        return 0

    lax.fori_loop(0, count // tile, encode, 0)

    kvy = []
    for d in range(1, npick):
        kvz[d].wait_recv()
        at = pl.ds(pl.multiple_of(zfrom[d] * rows + g * half, 16), half)
        kvy.append(go(put(kvw.at[at], kvw.at[at], kvy_s.at[d], kvy_r.at[d], mate)))
    own[0].wait()
    for c in kvy:
        c.wait_recv()

    def keys_values(i, _):
        at = pl.ds(pl.multiple_of(i * 256, 256), 256)
        kvs[at, :] = jnp.dot(enc[at, :], kvw[...], preferred_element_type=F32).astype(BF16)
        return 0

    lax.fori_loop(0, count // 256, keys_values, 0)

    lane = lax.broadcasted_iota(jnp.int32, (128, 128), 1)

    def cross_attention(i, _):
        at = pl.ds(pl.multiple_of(i * 128, 128), 128)
        mark = jnp.zeros((128, 128), F32)
        for h in range(nh):
            q = latents_ref[at, pl.ds(pl.multiple_of(col + h * HEAD, HEAD), HEAD)]
            s = lax.dot_general(q, kvs[:, h * HEAD : (h + 1) * HEAD], LAST, preferred_element_type=F32) * scale
            top = jnp.max(s, axis=1, keepdims=True)
            e = jnp.exp(s - top)
            total = jnp.sum(e, axis=1, keepdims=True)
            numer[at, h * HEAD : (h + 1) * HEAD] = jnp.dot(
                e.astype(BF16), kvs[:, local + h * HEAD : local + (h + 1) * HEAD], preferred_element_type=F32
            ).astype(BF16)
            mark = jnp.where(lane == 2 * h, top, jnp.where(lane == 2 * h + 1, total, mark))
        stats[at, :] = mark
        return 0

    lax.fori_loop(0, lat_rows // 128, cross_attention, 0)
    stin[0] = stats[...].T[:8]
    stz, nuz = [None], [None]
    for d in range(1, npick):
        dst = lax.rem(p + d, npick)
        stz.append(go(put(stin.at[0], stin.at[d], st_s.at[d], st_r.at[d], zto[d])))
        nuz.append(go(put(
            numer.at[pl.ds(pl.multiple_of(dst * share, 16), share)], parts.at[d],
            nu_s.at[d], nu_r.at[d], zto[d],
        )))
    dqy = []
    for d in range(1, npick):
        dqz[d].wait_recv()
        at = pl.ds(pl.multiple_of(zfrom[d] * rows + g * half, 16), half)
        dqy.append(go(put(dqw.at[at], dqw.at[at], dqy_s.at[d], dqy_r.at[d], mate)))
    for d in range(1, npick):
        stz[d].wait_recv()
    coef[...] = jnp.zeros(coef.shape, F32)
    for h in range(nh):
        best = stin[0, 2 * h : 2 * h + 1, :]
        for d in range(1, npick):
            best = jnp.maximum(best, stin[d, 2 * h : 2 * h + 1, :])
        factors = [jnp.exp(stin[d, 2 * h : 2 * h + 1, :] - best) for d in range(npick)]
        total = sum(factors[d] * stin[d, 2 * h + 1 : 2 * h + 2, :] for d in range(npick))
        for d in range(npick):
            coef[2 * d + h : 2 * d + h + 1, :] = factors[d] / total
    coeft[...] = coef[...].T
    myrows = pl.ds(pl.multiple_of(p * share, 16), share)
    factor = coeft[myrows, :]
    for d in range(1, npick):
        nuz[d].wait_recv()
    for h in range(nh):
        cols = slice(h * HEAD, (h + 1) * HEAD)
        acc = numer[myrows, cols].astype(F32) * factor[:, h : h + 1]
        for d in range(1, npick):
            acc += parts[d, :, cols].astype(F32) * factor[:, 2 * d + h : 2 * d + h + 1]
        att[myrows, pl.ds(pl.multiple_of(col + h * HEAD, HEAD), HEAD)] = acc.astype(BF16)
    mycols = pl.ds(col, local)
    azz = [None] + [
        go(put(att.at[myrows, mycols], att.at[myrows, mycols], az_s.at[d], az_r.at[d], zto[d]))
        for d in range(1, npick)
    ]
    ahh = []
    for d in range(npick):
        if d:
            azz[d].wait_recv()
        at = pl.ds(pl.multiple_of(zfrom[d] * share, 16), share)
        for e in range(1, nhead):
            k = d * nhead + e
            ahh.append(go(put(att.at[at, mycols], att.at[at, mycols], ah_s.at[k], ah_r.at[k], hto[e])))
    own[1].wait()
    for c in dqy:
        c.wait_recv()

    def queries(i, _):
        at = pl.ds(pl.multiple_of(i * 256, 256), 256)
        query[at, :] = jnp.dot(enc[at, :], dqw[...], preferred_element_type=F32).astype(BF16)
        return 0

    lax.fori_loop(0, count // 256, queries, 0)
    own[2].wait()
    for c in crh + ahh:
        c.wait_recv()

    def layer_in(i, _):
        at = pl.ds(pl.multiple_of(i * 128, 128), 128)
        x = latents_ref[at, :].astype(F32) + jnp.dot(att[at, :], cross[...], preferred_element_type=F32)
        state[at, :] = x
        power = jnp.mean(x * x, axis=1, keepdims=True)
        normed = (x * lax.rsqrt(power + EPS) * gains_ref[0:1, :]).astype(BF16)
        for j in range(3):
            qkv[j, at, :] = jnp.dot(normed, qkvw_ref[j], preferred_element_type=F32).astype(BF16)
        return 0

    lax.fori_loop(0, lat_rows // 128, layer_in, 0)

    def self_attention(i, _):
        at = pl.ds(pl.multiple_of(i * 128, 128), 128)
        for h in range(nh):
            cols = slice(h * HEAD, (h + 1) * HEAD)
            s = lax.dot_general(qkv[0, at, cols], qkv[1, :, cols], LAST, preferred_element_type=F32) * scale
            e = jnp.exp(s)
            probs = (e * (1.0 / jnp.sum(e, axis=1, keepdims=True))).astype(BF16)
            heads_all[at, pl.ds(pl.multiple_of(col + h * HEAD, HEAD), HEAD)] = jnp.dot(
                probs, qkv[2, :, cols], preferred_element_type=F32
            ).astype(BF16)
        return 0

    lax.fori_loop(0, lat_rows // 128, self_attention, 0)
    hoh = [
        go(put(heads_all.at[:, mycols], heads_all.at[:, mycols], ho_s.at[e], ho_r.at[e], hto[e]))
        for e in range(1, nhead)
    ]
    horizon = lax.broadcasted_iota(jnp.int32, (HORIZONS, count), 0)
    target = jnp.sum(jnp.where(horizon == ids_ref[...], levels_ref[...], 0.0), axis=0, keepdims=True)
    own[3].wait()
    for c in soh + hoh:
        c.wait_recv()

    def layer_out(i, _):
        at = pl.ds(pl.multiple_of(i * 128, 128), 128)
        x = state[at, :] + jnp.dot(heads_all[at, :], sout[...], preferred_element_type=F32)
        state[at, :] = x
        power = jnp.mean(x * x, axis=1, keepdims=True)
        normed = (x * lax.rsqrt(power + EPS) * gains_ref[1:2, :]).astype(BF16)
        dkeys[at, :] = jnp.dot(normed, deckv_ref[0], preferred_element_type=F32).astype(BF16)
        vals = jnp.dot(normed, deckv_ref[1], preferred_element_type=F32).astype(BF16).astype(F32)
        vals = vals * readout_ref[...]
        mark = jnp.zeros((128, 128), F32)
        for h in range(nh):
            mark = jnp.where(
                lane == h, jnp.sum(vals[:, h * HEAD : (h + 1) * HEAD], axis=1, keepdims=True), mark
            )
        vread[at, :] = mark
        return 0

    lax.fori_loop(0, lat_rows // 128, layer_out, 0)
    latout_ref[...] = state[:, mycols]
    dkeyst[...] = dkeys[...].astype(F32).T.astype(BF16)

    def decode(i, _):
        at = pl.ds(pl.multiple_of(i * 256, 256), 256)
        mine = jnp.zeros((1, 256), F32)
        for h in range(nh):
            cols = slice(h * HEAD, (h + 1) * HEAD)
            s = lax.dot_general(dkeys[:, cols], query[at, cols], LAST, preferred_element_type=F32) * scale
            e = jnp.exp(s)
            w = e * (1.0 / jnp.sum(e, axis=0, keepdims=True))
            v = vread[:, h : h + 1]
            f = jnp.sum(w * v, axis=0, keepdims=True)
            mine += f
            dqt[cols, at] = jnp.dot(
                dkeyst[cols, :], (w * (v - f)).astype(BF16), preferred_element_type=F32
            )
        fpart[:, at] = jnp.broadcast_to(mine, (8, 256))
        return 0

    lax.fori_loop(0, count // 256, decode, 0)
    fdh = [
        go(put(fpart, fin.at[e], fd_s.at[e], fd_r.at[e], hto[e])) for e in range(1, nhead)
    ]
    for c in fdh:
        c.wait_recv()
    field = fpart[0:1, :]
    for e in range(1, nhead):
        field = field + fin[e, 0:1, :]
    field_ref[...] = field
    dqb[...] = (dqt[...] * ((field - target) * scale)).astype(BF16)

    def gradient(i, _):
        at = pl.ds(pl.multiple_of(i * 512, 512), 512)
        out = jnp.dot(dqb[...], enc[:, at], preferred_element_type=F32)
        gbuf[at, :] = out.T.astype(BF16)
        return 0

    lax.fori_loop(0, features // 512, gradient, 0)
    grz = [
        go(put(
            gbuf.at[pl.ds(pl.multiple_of(lax.rem(p + d, npick) * rows, 16), rows)], gin.at[d],
            gr_s.at[d], gr_r.at[d], zto[d],
        ))
        for d in range(1, npick)
    ]
    for c in grz:
        c.wait_recv()
    total = gbuf[pl.ds(mine, rows), :].astype(F32)
    for d in range(1, npick):
        total += gin[d].astype(F32)
    grad_ref[...] = total
    for c in sends:
        c.wait_send()


def on_device(
    npick, nhead, coords, horizon_ids, horizon_levels, latents, kv_weight, cross_out, norm_gains,
    self_qkv, self_out, dec_kv, dec_query, readout,
):
    count = coords.shape[1]
    rows, local = dec_query.shape
    lat_rows, width = latents.shape
    features = rows * npick
    share = lat_rows // npick
    wide = -(-2 * npick // 128) * 128
    freq = (0.5 * jnp.linspace(1.0, BANDS / 2.0, BANDS).astype(F32)).reshape(1, BANDS)
    vmem = pl.BlockSpec(memory_space=pltpu.VMEM)
    hbm = pl.BlockSpec(memory_space=pl.ANY)
    dma = lambda n: pltpu.SemaphoreType.DMA((n,))
    scratch = [
        pltpu.VMEM((count, features), BF16),
        pltpu.VMEM((features, 2 * local), BF16),
        pltpu.VMEM((features, local), BF16),
        pltpu.VMEM((width, width), BF16),
        pltpu.VMEM((width, width), BF16),
        pltpu.VMEM((count, 2 * local), BF16),
        pltpu.VMEM((lat_rows, local), BF16),
        pltpu.VMEM((lat_rows, 128), F32),
        pltpu.VMEM((npick, 8, lat_rows), F32),
        pltpu.VMEM((npick, share, local), BF16),
        pltpu.VMEM((wide, lat_rows), F32),
        pltpu.VMEM((lat_rows, wide), F32),
        pltpu.VMEM((lat_rows, width), BF16),
        pltpu.VMEM((lat_rows, width), F32),
        pltpu.VMEM((3, lat_rows, local), BF16),
        pltpu.VMEM((lat_rows, width), BF16),
        pltpu.VMEM((lat_rows, local), BF16),
        pltpu.VMEM((local, lat_rows), BF16),
        pltpu.VMEM((lat_rows, 128), F32),
        pltpu.VMEM((count, local), BF16),
        pltpu.VMEM((local, count), F32),
        pltpu.VMEM((local, count), BF16),
        pltpu.VMEM((8, count), F32),
        pltpu.VMEM((nhead, 8, count), F32),
        pltpu.VMEM((features, local), BF16),
        pltpu.VMEM((npick, rows, local), BF16),
    ]
    z, h = npick, nhead
    for n in (z, z, z, z, h, h, z, z, z, z * h, h, h, z):
        scratch += [dma(n), dma(n)]
    scratch.append(dma(4))
    field, latents_out, grad = pl.pallas_call(
        functools.partial(kernel, npick, nhead),
        out_shape=(
            jax.ShapeDtypeStruct((1, count), F32),
            jax.ShapeDtypeStruct((lat_rows, local), F32),
            jax.ShapeDtypeStruct((rows, local), F32),
        ),
        in_specs=[vmem] * 5 + [hbm, hbm, vmem, vmem, hbm, vmem, hbm, vmem],
        out_specs=(vmem, vmem, vmem),
        scratch_shapes=scratch,
        compiler_params=pltpu.CompilerParams(
            collective_id=0, has_side_effects=True, vmem_limit_bytes=56 * 2**20
        ),
    )(
        coords.T,
        horizon_ids.reshape(1, count),
        horizon_levels.reshape(-1, 1),
        freq,
        latents,
        kv_weight.reshape(rows, 2 * local),
        cross_out,
        norm_gains,
        self_qkv,
        self_out,
        dec_kv,
        dec_query,
        readout.reshape(1, local),
    )
    return field.reshape(count), latents_out, grad


def solution(mesh):
    in_specs = (
        P(None, ("groups", "picks")),
        P(("groups", "picks")),
        P("groups"),
        P(),
        P("picks", None, "heads"),
        P("heads", None),
        P(),
        P(None, None, "heads"),
        P(None, "heads"),
        P(None, None, "heads"),
        P("picks", "heads"),
        P("heads"),
    )
    out_specs = (P(("groups", "picks")), P("groups", "heads"), P(("groups", "picks"), "heads"))
    return jax.shard_map(
        functools.partial(on_device, mesh.shape["picks"], mesh.shape["heads"]),
        mesh=mesh, in_specs=in_specs, out_specs=out_specs, check_vma=False,
    )
```

time: 320 us -> 175 us (0.55)
  waiting for transfers between devices: 192 us -> 0 us
  Pallas kernels: 0 us -> 164 us
  other arithmetic: 40.5 us -> 0.66 us
  blocking collectives: 32.4 us -> 0 us
  matrix products: 29.1 us -> 0 us
  between operations: 14.4 us -> 0.65 us
    pallas_call x0 -> x1, Pallas kernels: none -> 164 us  [on_device(): pl.pallas_call(functools.partial(kernel, npick, nhead), out_shape=(jax.Sh...]
    all_gather x4 -> x0, waiting for transfers between devices: 94.8 us -> none  [the longest x1 36 us: on_device(): piece = lax.all_gather(kv_weight, 'picks', axis=0, tiled=True)]
    psum x2 -> x0, waiting for transfers between devices: 61.1 us -> none  [the longest x1 35.8 us: on_device(): lax.psum(partial_value.astype(jnp.bfloat16), 'heads').astype(jnp.float32)]
    reduce_scatter x1 -> x0, waiting for transfers between devices: 35.2 us -> none  [on_device(): lax.psum_scatter(jnp.dot(rows.T, dquery, preferred_element_type=jnp.float...]
    dot_general x15 -> x0, matrix products: 29.1 us -> none  [the longest x1 5.05 us: on_device(): jnp.dot(rows, lax.all_gather(dec_query, 'picks', axis=0, tiled=True), pre...]
    another operation x1 -> x0, other arithmetic: 23.6 us -> none
    psum x3 -> x0, blocking collectives: 21.2 us -> none  [the longest x1 9.12 us: on_device(): lax.psum((total * factor).astype(jnp.bfloat16), 'picks').astype(jnp.float32)]
    pmax x1 -> x0, blocking collectives: 11.2 us -> none  [on_device(): best = lax.pmax(top, 'picks')]
  transfers between devices with their start and end apart: 7 -> 0, of which waited for: 7 -> 0; matrix products, arithmetic and copies ran while one was open for 11% -> 0% of each run, Pallas kernels for 0% -> 0%
where the time goes in v1:
time: 175 us
  Pallas kernels  164 us (94%)
  local copies, waits for them, and re-layouts  9.35 us (5%)
    pallas_call x1, Pallas kernels, on_device(): pl.pallas_call(functools.partial(kernel, npick, nhead), out_shape=(jax.Sh...  164 us
    unnamed x7, local copies, waits for them, and re-layouts  8.01 us

profile of v1, /device:TPU:8, one launch (start us, length us, event | category | flops | bytes accessed | tf_op | source)
XLA Modules:
  0.0 174.6 jit_solution(9644222429090876386)
XLA Ops:
  0.6 0.7 maximum_multiply_fusion.freq_ref
  1.3 1.3 copy.16.levels_ref
  2.6 1.7 copy.15
  4.4 2.2 %copy.17 = bf16[96,8,2,256]{3,1,2,0:T(8,128)(2,1)} copy(bf16[96,8,2,256]{3,2,1,0:T(2,128)(2,1)} %bitcast.10) | data formatting | bytes 1572864
  6.6 164.0 %shard_map.139 = (f32[1,1024]{1,0:T(1,128)}, f32[512,256]{1,0:T(8,128)}, f32[768,256]{1,0:T(8,128)}) custom-call(f32[1024,3]{1,0:T(8,128)} %bitcast.9, s32[1,1024]{1,0:T(1,128)} %bitcast.13, f32[64,1]{1,0:T(8,128)} %copy.16.levels_ref, f32[1,512]{1,0:T(1,128)} %maximum_multiply_fusion.freq_ref, bf16[512,1024]{1,0:T(8,128)(2,1)} %latents_ref.1, ...), custom_call_target="tpu_custom_call" | custom-call | tf_op jit(solution)/shard_map/pallas_call | solution.py:380
  170.5 0.0 copy-start
  170.5 1.3 copy.21
  171.9 1.9 %copy.22 = f32[512,256]{1,0:T(8,128)} copy(f32[512,256]{1,0:T(8,128)} %get-tuple-element.13) | data formatting | bytes 1048576
  173.7 0.0 copy-done
  173.7 0.9 copy.23
  (1 shorter events, 0.0 us)
Async XLA Ops:
  170.5 3.2 %copy-start = (f32[768,256]{1,0:T(8,128)S(1)}, f32[768,256]{1,0:T(8,128)}, u32[]{:S(2)}) copy-start(f32[768,256]{1,0:T(8,128)} %get-tuple-element.14) | copy-start | bytes 2359300

commit v2 on v1

--- a/solution.py
+++ b/solution.py
@@ -41,9 +41,9 @@
     qkvw_ref, sout_in, deckv_ref, dq_in, readout_ref,
     field_ref, latout_ref, grad_ref,
     enc, kvw, dqw, cross, sout, kvs, numer, stats, stin, parts, coef, coeft, att, state,
-    qkv, heads_all, dkeys, dkeyst, vread, query, dqt, dqb, fpart, fin, gbuf, gin,
-    kv_s, kv_r, kvy_s, kvy_r, dq_s, dq_r, dqy_s, dqy_r, cr_s, cr_r, so_s, so_r,
-    nu_s, nu_r, st_s, st_r, az_s, az_r, ah_s, ah_r, ho_s, ho_r, fd_s, fd_r, gr_s, gr_r, loc,
+    qkv, heads_all, dkeys, dkeyst, vread, query, dqt, dqb, fpart, fin, gbuf, gin, gin_left, expo,
+    wz_s, wz_r, wy_s, wy_r, cr_s, cr_r, so_s, so_r,
+    nu_s, nu_r, st_s, st_r, az_s, az_r, ah_s, ah_r, ho_s, ho_r, fd_s, fd_r, gr_s, gr_r, gl_r, loc,
 ):
     g = lax.axis_index("groups")
     p = lax.axis_index("picks")
@@ -89,12 +89,89 @@
         pl.semaphore_signal(barrier, inc=1, device_id=to, device_id_type=pl.DeviceIdType.MESH)
     pl.semaphore_wait(barrier, npick + nhead - 1)
 
-    myhalf = pl.multiple_of(g * half, 16)
-    dst_half = pl.ds(pl.multiple_of(p * rows + g * half, 16), half)
-    kvz = [None] + [
-        go(put(kv_in.at[pl.ds(myhalf, half)], kvw.at[dst_half], kv_s.at[d], kv_r.at[d], zto[d]))
-        for d in range(1, npick)
-    ]
+    spots = [(kv_in, kvw, 0), (kv_in, kvw, local), (dq_in, dqw, 0)]
+    ahead = [{"picks": jnp.minimum(p + 1, npick - 1)}, {"picks": jnp.maximum(p - 1, 0)}]
+    may = [p + 1 < npick, p > 0]
+
+    def span(owner, part):
+        return pl.ds(pl.multiple_of(owner * rows + part * half, 16), half)
+
+    def along(c, way, s):
+        _, whole, first = spots[c]
+        owner = p - s if way == 0 else p + s
+        ref = whole.at[span(owner, g), pl.ds(first, local)]
+        k = (c * 2 + way) * npick + s
+        return put(ref, ref, wz_s.at[k], wz_r.at[k + 1], ahead[way])
+
+    def start_own(c):
+        source, whole, first = spots[c]
+        for way in range(2):
+            k = (c * 2 + way) * npick
+
+            @pl.when(may[way])
+            def _():
+                put(
+                    source.at[pl.ds(pl.multiple_of(g * half, 16), half), pl.ds(first, local)],
+                    whole.at[span(p, g), pl.ds(first, local)],
+                    wz_s.at[k], wz_r.at[k + 1], ahead[way],
+                ).start()
+
+    def across(c, way, s):
+        _, whole, first = spots[c]
+        owner = p - s if way == 0 else p + s
+        ref = whole.at[span(owner, g), pl.ds(first, local)]
+        k = (c * 2 + way) * npick + s
+        return put(ref, ref, wy_s.at[k], wy_r.at[k], mate)
+
+    def has(way, s):
+        return p - s >= 0 if way == 0 else p + s < npick
+
+    def pass_on(c, s):
+        _, whole, first = spots[c]
+        for way in range(2):
+
+            @pl.when(has(way, s))
+            def _():
+                owner = p - s if way == 0 else p + s
+                ref = whole.at[span(owner, g), pl.ds(first, local)]
+                k = (c * 2 + way) * npick + s
+                put(ref, ref, wz_s.at[k], wz_r.at[k], mate).wait_recv()
+                across(c, way, s).start()
+
+                if s < npick - 1:
+
+                    @pl.when(may[way])
+                    def _():
+                        along(c, way, s).start()
+
+    def pass_on_rest(c):
+        for s in range(3, npick):
+            pass_on(c, s)
+
+    def arrive(c):
+        for s in range(1, npick):
+            for way in range(2):
+
+                @pl.when(has(way, s))
+                def _():
+                    across(c, way, s).wait_recv()
+
+    def finish(c):
+        for s in range(npick):
+            for way in range(2):
+                if s < npick - 1:
+
+                    @pl.when(has(way, s) & may[way])
+                    def _():
+                        along(c, way, s).wait_send()
+
+                if s:
+
+                    @pl.when(has(way, s))
+                    def _():
+                        across(c, way, s).wait_send()
+
+    start_own(0)
     crh = [
         go(put(cross_in, cross.at[pl.ds(col, local)], cr_s.at[e], cr_r.at[e], hto[e]))
         for e in range(1, nhead)
@@ -102,10 +179,6 @@
     soh = [
         go(put(sout_in, sout.at[:, pl.ds(col, local)], so_s.at[e], so_r.at[e], hto[e]))
         for e in range(1, nhead)
-    ]
-    dqz = [None] + [
-        go(put(dq_in.at[pl.ds(myhalf, half)], dqw.at[dst_half], dq_s.at[d], dq_r.at[d], zto[d]))
-        for d in range(1, npick)
     ]
 
     tile = 32
@@ -122,27 +195,37 @@
             enc[at, (3 + c) * BANDS : (4 + c) * BANDS] = (1.0 - 2.0 * s * s).astype(BF16)
         return 0
 
-    lax.fori_loop(0, count // tile, encode, 0)
-
-    kvy = []
-    for d in range(1, npick):
-        kvz[d].wait_recv()
-        at = pl.ds(pl.multiple_of(zfrom[d] * rows + g * half, 16), half)
-        kvy.append(go(put(kvw.at[at], kvw.at[at], kvy_s.at[d], kvy_r.at[d], mate)))
+    steps = count // tile
+    lax.fori_loop(0, steps // 3, encode, 0)
+    pass_on(0, 1)
+    start_own(1)
+    lax.fori_loop(steps // 3, 2 * steps // 3, encode, 0)
+    if npick > 2:
+        pass_on(0, 2)
+    lax.fori_loop(2 * steps // 3, steps, encode, 0)
+    pass_on_rest(0)
+    pass_on(1, 1)
+    start_own(2)
     own[0].wait()
-    for c in kvy:
-        c.wait_recv()
-
-    def keys_values(i, _):
-        at = pl.ds(pl.multiple_of(i * 256, 256), 256)
-        kvs[at, :] = jnp.dot(enc[at, :], kvw[...], preferred_element_type=F32).astype(BF16)
-        return 0
-
-    lax.fori_loop(0, count // 256, keys_values, 0)
+    arrive(0)
+
+    def project(first):
+        def body(i, _):
+            at = pl.ds(pl.multiple_of(i * 256, 256), 256)
+            kvs[at, first : first + local] = jnp.dot(
+                enc[at, :], kvw[:, first : first + local], preferred_element_type=F32
+            ).astype(BF16)
+            return 0
+
+        lax.fori_loop(0, count // 256, body, 0)
+
+    project(0)
+    if npick > 2:
+        pass_on(1, 2)
 
     lane = lax.broadcasted_iota(jnp.int32, (128, 128), 1)
 
-    def cross_attention(i, _):
+    def cross_scores(i, _):
         at = pl.ds(pl.multiple_of(i * 128, 128), 128)
         mark = jnp.zeros((128, 128), F32)
         for h in range(nh):
@@ -151,28 +234,39 @@
             top = jnp.max(s, axis=1, keepdims=True)
             e = jnp.exp(s - top)
             total = jnp.sum(e, axis=1, keepdims=True)
-            numer[at, h * HEAD : (h + 1) * HEAD] = jnp.dot(
-                e.astype(BF16), kvs[:, local + h * HEAD : local + (h + 1) * HEAD], preferred_element_type=F32
-            ).astype(BF16)
+            expo[h, at, :] = e.astype(BF16)
             mark = jnp.where(lane == 2 * h, top, jnp.where(lane == 2 * h + 1, total, mark))
         stats[at, :] = mark
         return 0
 
-    lax.fori_loop(0, lat_rows // 128, cross_attention, 0)
+    lax.fori_loop(0, lat_rows // 128, cross_scores, 0)
+    pass_on_rest(1)
     stin[0] = stats[...].T[:8]
     stz, nuz = [None], [None]
     for d in range(1, npick):
+        stz.append(go(put(stin.at[0], stin.at[d], st_s.at[d], st_r.at[d], zto[d])))
+    pass_on(2, 1)
+    arrive(1)
+    project(local)
+    if npick > 2:
+        pass_on(2, 2)
+
+    def cross_values(i, _):
+        at = pl.ds(pl.multiple_of(i * 128, 128), 128)
+        for h in range(nh):
+            numer[at, h * HEAD : (h + 1) * HEAD] = jnp.dot(
+                expo[h, at, :], kvs[:, local + h * HEAD : local + (h + 1) * HEAD], preferred_element_type=F32
+            ).astype(BF16)
+        return 0
+
+    lax.fori_loop(0, lat_rows // 128, cross_values, 0)
+    for d in range(1, npick):
         dst = lax.rem(p + d, npick)
-        stz.append(go(put(stin.at[0], stin.at[d], st_s.at[d], st_r.at[d], zto[d])))
         nuz.append(go(put(
             numer.at[pl.ds(pl.multiple_of(dst * share, 16), share)], parts.at[d],
             nu_s.at[d], nu_r.at[d], zto[d],
         )))
-    dqy = []
-    for d in range(1, npick):
-        dqz[d].wait_recv()
-        at = pl.ds(pl.multiple_of(zfrom[d] * rows + g * half, 16), half)
-        dqy.append(go(put(dqw.at[at], dqw.at[at], dqy_s.at[d], dqy_r.at[d], mate)))
+    pass_on_rest(2)
     for d in range(1, npick):
         stz[d].wait_recv()
     coef[...] = jnp.zeros(coef.shape, F32)
@@ -209,8 +303,7 @@
             k = d * nhead + e
             ahh.append(go(put(att.at[at, mycols], att.at[at, mycols], ah_s.at[k], ah_r.at[k], hto[e])))
     own[1].wait()
-    for c in dqy:
-        c.wait_recv()
+    arrive(2)
 
     def queries(i, _):
         at = pl.ds(pl.multiple_of(i * 256, 256), 256)
@@ -314,19 +407,55 @@
         return 0
 
     lax.fori_loop(0, features // 512, gradient, 0)
-    grz = [
-        go(put(
-            gbuf.at[pl.ds(pl.multiple_of(lax.rem(p + d, npick) * rows, 16), rows)], gin.at[d],
-            gr_s.at[d], gr_r.at[d], zto[d],
-        ))
-        for d in range(1, npick)
-    ]
-    for c in grz:
-        c.wait_recv()
-    total = gbuf[pl.ds(mine, rows), :].astype(F32)
-    for d in range(1, npick):
-        total += gin[d].astype(F32)
-    grad_ref[...] = total
+
+    def partial(q, c, way):
+        k = q * 2 + c
+        at = pl.ds(q * rows + c * half, half)
+        into, sem = (gin, gr_r) if way == 0 else (gin_left, gl_r)
+        return put(gbuf.at[at], into.at[q, pl.ds(c * half, half)], gr_s.at[k], sem.at[k], ahead[way])
+
+    def onward(q, c, way):
+        at = slice(q * rows + c * half, q * rows + (c + 1) * half)
+
+        @pl.when(has(way, 1))
+        def _():
+            partial(q, c, way).wait_recv()
+            gbuf[at, :] = (
+                gbuf[at, :].astype(F32) + (gin, gin_left)[way][q, c * half : (c + 1) * half, :].astype(F32)
+            ).astype(BF16)
+
+        partial(q, c, way).start()
+
+    for k in range(npick - 1):
+        for c in range(2):
+            for way in range(2):
+                q = npick - 1 - k if way == 0 else k
+
+                @pl.when(p < q if way == 0 else p > q)
+                def _():
+                    onward(q, c, way)
+
+    grad_ref[...] = gbuf[pl.ds(mine, rows), :].astype(F32)
+    for way in range(2):
+
+        @pl.when(has(way, 1))
+        def _():
+            for c in range(2):
+                k = p * 2 + c
+                at = pl.ds(c * half, half)
+                ref = (gin if way == 0 else gin_left).at[p, at]
+                put(ref, ref, gr_s.at[k], (gr_r if way == 0 else gl_r).at[k], mate).wait_recv()
+                grad_ref[at, :] += ref[...].astype(F32)
+
+    for q in range(npick):
+        for c in range(2):
+
+            @pl.when(p != q)
+            def _():
+                partial(q, c, 0).wait_send()
+
+    for c in range(3):
+        finish(c)
     for c in sends:
         c.wait_send()
 
@@ -372,11 +501,13 @@
         pltpu.VMEM((nhead, 8, count), F32),
         pltpu.VMEM((features, local), BF16),
         pltpu.VMEM((npick, rows, local), BF16),
+        pltpu.VMEM((npick, rows, local), BF16),
+        pltpu.VMEM((local // HEAD, lat_rows, count), BF16),
     ]
     z, h = npick, nhead
-    for n in (z, z, z, z, h, h, z, z, z, z * h, h, h, z):
+    for n in (6 * z, 6 * z, h, h, z, z, z, z * h, h, h, 2 * z):
         scratch += [dma(n), dma(n)]
-    scratch.append(dma(4))
+    scratch += [dma(2 * z), dma(4)]
     field, latents_out, grad = pl.pallas_call(
         functools.partial(kernel, npick, nhead),
         out_shape=(

time: 175 us -> 149 us (0.85)
  Pallas kernels: 164 us -> 137 us
    pallas_call x1, Pallas kernels: 164 us -> 137 us  [on_device(): pl.pallas_call(functools.partial(kernel, npick, nhead), out_shape=(jax.Sh...]
where the time goes in v2:
time: 149 us; the launch traced here: 148 us
  Pallas kernels  137 us (92%)
  local copies, waits for them, and re-layouts  9.35 us (6%)
    pallas_call x1, Pallas kernels, on_device(): pl.pallas_call(functools.partial(kernel, npick, nhead), out_shape=(jax.Sh...  137 us
    unnamed x7, local copies, waits for them, and re-layouts  8.01 us

profile of v2, /device:TPU:8, one launch (start us, length us, event | category | flops | bytes accessed | tf_op | source)
XLA Modules:
  0.0 147.7 jit_solution(16738120341339764384)
XLA Ops:
  0.6 0.7 maximum_multiply_fusion.freq_ref
  1.3 1.3 copy.16.levels_ref
  2.6 1.7 %copy.15 = f32[3,1024]{0,1:T(8,128)} copy(f32[3,1024]{1,0:T(4,128)} %param.12) | data formatting | bytes 24576 | tf_op args[0]
  4.4 2.2 %copy.17 = bf16[96,8,2,256]{3,1,2,0:T(8,128)(2,1)} copy(bf16[96,8,2,256]{3,2,1,0:T(2,128)(2,1)} %bitcast.10) | data formatting | bytes 1572864
  6.6 137.1 %shard_map.139 = (f32[1,1024]{1,0:T(1,128)}, f32[512,256]{1,0:T(8,128)}, f32[768,256]{1,0:T(8,128)}) custom-call(f32[1024,3]{1,0:T(8,128)} %bitcast.9, s32[1,1024]{1,0:T(1,128)} %bitcast.13, f32[64,1]{1,0:T(8,128)} %copy.16.levels_ref, f32[1,512]{1,0:T(1,128)} %maximum_multiply_fusion.freq_ref, bf16[512,1024]{1,0:T(8,128)(2,1)} %latents_ref.1, ...), custom_call_target="tpu_custom_call" | custom-call | tf_op jit(solution)/shard_map/pallas_call | solution.py:511
  143.6 0.0 copy-start
  143.7 1.3 copy.21
  145.0 1.9 %copy.22 = f32[512,256]{1,0:T(8,128)} copy(f32[512,256]{1,0:T(8,128)} %get-tuple-element.13) | data formatting | bytes 1048576
  146.9 0.0 copy-done
  146.9 0.9 copy.23
  (1 shorter events, 0.0 us)
Async XLA Ops:
  143.6 3.2 %copy-start = (f32[768,256]{1,0:T(8,128)S(1)}, f32[768,256]{1,0:T(8,128)}, u32[]{:S(2)}) copy-start(f32[768,256]{1,0:T(8,128)} %get-tuple-element.14) | copy-start | bytes 2359300

commit v3 on v2

--- a/solution.py
+++ b/solution.py
@@ -406,7 +406,19 @@
         gbuf[at, :] = out.T.astype(BF16)
         return 0
 
-    lax.fori_loop(0, features // 512, gradient, 0)
+    by_block = rows % 256 == 0
+    if not by_block:
+        lax.fori_loop(0, features // 512, gradient, 0)
+
+    def gradient_block(q):
+        def body(i, _):
+            at = pl.ds(pl.multiple_of(q * rows + i * 256, 256), 256)
+            out = jnp.dot(dqb[...], enc[:, at], preferred_element_type=F32)
+            gbuf[at, :] = out.T.astype(BF16)
+            return 0
+
+        if by_block:
+            lax.fori_loop(0, rows // 256, body, 0)
 
     def partial(q, c, way):
         k = q * 2 + c
@@ -433,8 +445,11 @@
 
                 @pl.when(p < q if way == 0 else p > q)
                 def _():
+                    if c == 0:
+                        gradient_block(q)
                     onward(q, c, way)
 
+    gradient_block(p)
     grad_ref[...] = gbuf[pl.ds(mine, rows), :].astype(F32)
     for way in range(2):
 

time: 149 us -> 150 us (level)
  no operation moved by 1% of the time
where the time goes in v3:
time: 150 us; the launch traced here: 148 us
  Pallas kernels  137 us (91%)
  local copies, waits for them, and re-layouts  9.35 us (6%)
    pallas_call x1, Pallas kernels, on_device(): pl.pallas_call(functools.partial(kernel, npick, nhead), out_shape=(jax.Sh...  137 us
    unnamed x7, local copies, waits for them, and re-layouts  8.01 us

profile of v3, /device:TPU:8, one launch (start us, length us, event | category | flops | bytes accessed | tf_op | source)
XLA Modules:
  0.0 148.2 jit_solution(894794048807812260)
XLA Ops:
  0.6 0.7 maximum_multiply_fusion.freq_ref
  1.3 1.3 copy.16.levels_ref
  2.6 1.7 %copy.15 = f32[3,1024]{0,1:T(8,128)} copy(f32[3,1024]{1,0:T(4,128)} %param.12) | data formatting | bytes 24576 | tf_op args[0]
  4.4 2.2 %copy.17 = bf16[96,8,2,256]{3,1,2,0:T(8,128)(2,1)} copy(bf16[96,8,2,256]{3,2,1,0:T(2,128)(2,1)} %bitcast.10) | data formatting | bytes 1572864
  6.6 137.5 %shard_map.139 = (f32[1,1024]{1,0:T(1,128)}, f32[512,256]{1,0:T(8,128)}, f32[768,256]{1,0:T(8,128)}) custom-call(f32[1024,3]{1,0:T(8,128)} %bitcast.9, s32[1,1024]{1,0:T(1,128)} %bitcast.13, f32[64,1]{1,0:T(8,128)} %copy.16.levels_ref, f32[1,512]{1,0:T(1,128)} %maximum_multiply_fusion.freq_ref, bf16[512,1024]{1,0:T(8,128)(2,1)} %latents_ref.1, ...), custom_call_target="tpu_custom_call" | custom-call | tf_op jit(solution)/shard_map/pallas_call | solution.py:526
  144.1 0.0 copy-start
  144.1 1.3 copy.21
  145.4 1.9 %copy.22 = f32[512,256]{1,0:T(8,128)} copy(f32[512,256]{1,0:T(8,128)} %get-tuple-element.13) | data formatting | bytes 1048576
  147.3 0.0 copy-done
  147.3 0.9 copy.23
  (1 shorter events, 0.0 us)
Async XLA Ops:
  144.1 3.2 %copy-start = (f32[768,256]{1,0:T(8,128)S(1)}, f32[768,256]{1,0:T(8,128)}, u32[]{:S(2)}) copy-start(f32[768,256]{1,0:T(8,128)} %get-tuple-element.14) | copy-start | bytes 2359300
